TPU v7x, 32 devices: a whole 2x2x4 slice. The times are simulated.
32 devices in a mesh: row: 4 (over y, x), col: 8 (over z, core).
Axes of the slice: x: 2, y: 2, z: 4, core: 2. Of those that a mesh axis runs over, the one named last changes fastest.
Arguments:
- inputs: bfloat16 [512, 12288], P('col', 'row'), may hold values from -6 to 6
- in_weight: bfloat16 [12288, 24576], P('row', 'col'), may hold values from -0.0546875 to 0.0546875
- in_bias: float32 [24576], P('col'), may hold values from -3 to 3
- out_weight: bfloat16 [24576, 12288], P('col', 'row'), may hold values from -0.0390625 to 0.0390625
- out_bias: float32 [12288], P('row'), may hold values from -3 to 3
- cotangent: bfloat16 [512, 12288], P('col', 'row'), may hold values from -1.5 to 1.5
Outputs:
- output: bfloat16 [512, 12288], P('col', 'row')
- input_grad: bfloat16 [512, 12288], P('col', 'row')
- in_weight_grad: bfloat16 [12288, 24576], P('row', 'col')
- out_weight_grad: bfloat16 [24576, 12288], P('col', 'row')
- in_bias_grad: float32 [24576], P('col')
- out_bias_grad: float32 [12288], P('row')
All inputs are finite; a program needn't handle non-finite values.
Results may differ from a plain program's by a relative error of at most 0.0049.
Values may be sent and summed in bfloat16 or wider, within the bound.
No kernel may reach another device: no remote copies, remote signals or barrier semaphores. Data moves between devices by JAX's collectives and lax.ppermute only.
A program may use at most 192 MiB of HBM per device.

v0:
```python
import math

import jax
import jax.numpy as jnp
from jax import lax
from jax.experimental import pallas as pl
from jax.experimental.pallas import tpu as pltpu
from jax.sharding import PartitionSpec as P

root_two_pi = math.sqrt(2.0 / math.pi)
bf16 = jnp.bfloat16
f32 = jnp.float32


def gelu_both(value):
    inner = jnp.tanh(root_two_pi * (value + 0.044715 * value * value * value))
    hidden = 0.5 * value * (1.0 + inner)
    slope = 0.5 * (1.0 + inner) + 0.5 * value * (1.0 - inner * inner) * root_two_pi * (
        1.0 + 3.0 * 0.044715 * value * value
    )
    return hidden, slope


class Links:
    def __init__(self, rows, cols):
        self.rows, self.cols, self.chips = rows, cols, cols // 2
        self.phases = rows.bit_length() - 1
        ring = list(range(0, self.chips, 2)) + list(range(1, self.chips, 2))[::-1]
        self.ring_pairs = [
            (ring[i] * 2 + core, ring[(i + 1) % self.chips] * 2 + core)
            for i in range(self.chips)
            for core in range(2)
        ]
        self.core_pairs = [(i, i ^ 1) for i in range(cols)]
        self.orders = [
            [(phase + core) % self.phases for phase in range(self.phases)] for core in range(2)
        ]

    def ring(self, value):
        return lax.ppermute(value, "col", self.ring_pairs)

    def swap(self, value):
        return lax.ppermute(value, "col", self.core_pairs)

    def exchange(self, value, phase):
        pairs = [
            (row * self.cols + col, (row ^ (1 << self.orders[col % 2][phase])) * self.cols + col)
            for row in range(self.rows)
            for col in range(self.cols)
        ]
        return lax.ppermute(value, ("row", "col"), pairs)

    def flips(self, position):
        return [
            sum(
                ((position >> (self.phases - 1 - phase)) & 1) << order[phase]
                for phase in range(self.phases)
            )
            for order in self.orders
        ]

    def block_at(self, position):
        row, core = lax.axis_index("row"), lax.axis_index("col") % 2
        flip = self.flips(position)
        return row ^ jnp.where(core == 0, flip[0], flip[1])

    def position_of(self, block):
        flip = lax.axis_index("row") ^ block
        core = lax.axis_index("col") % 2
        place = [
            sum(((flip >> bit) & 1) << (self.phases - 1 - phase) for phase, bit in enumerate(order))
            for order in self.orders
        ]
        return jnp.where(core == 0, place[0], place[1])


def then(value, *others):
    return lax.optimization_barrier((value, *others))[0]


class Order:
    def __init__(self):
        self.token = None

    def gate(self, value):
        return value if self.token is None else then(value, self.token)

    def mark(self, *values):
        self.token = then(self.token, *values)

    def run(self, call, *operands):
        *results, self.token = call(*operands, [] if self.token is None else [self.token])
        return results


def pause(flops, after):
    def kernel(*refs):
        refs[-1][...] = jnp.zeros_like(refs[-1])

    return pl.pallas_call(
        kernel,
        in_specs=[ANY] * len(after),
        out_specs=[VMEM],
        out_shape=[TOKEN],
        compiler_params=params(1),
        name="pause",
        cost_estimate=pl.CostEstimate(flops=flops, bytes_accessed=1024, transcendentals=0),
    )(*after)


class RowSum:
    def __init__(self, links, order, keep, send):
        self.links, self.order, self.keep, self.phase = links, order, keep, 0
        self.pending = links.exchange(send, 0)

    def middle(self):
        for phase in range(1, self.links.phases):
            total = self.keep + self.order.gate(self.pending).astype(f32)
            half = total.shape[0] // 2
            self.keep, send = total[:half], total[half:].astype(bf16)
            self.order.mark(send)
            self.pending = self.links.exchange(send, phase)

    def finish(self):
        return self.keep + self.order.gate(self.pending).astype(f32)


class RowGather:
    def __init__(self, links, order, value):
        self.links, self.order, self.pieces = links, order, [value]
        order.mark(value)
        self.pending = links.exchange(value, links.phases - 1)

    def middle(self):
        for phase in reversed(range(self.links.phases - 1)):
            self.pieces.append(self.order.gate(self.pending))
            whole = jnp.concatenate(self.pieces)
            self.order.mark(whole)
            self.pending = self.links.exchange(whole, phase)

    def finish(self):
        return self.pieces + [self.order.gate(self.pending)]


class ChipSum:
    def __init__(self, links, order):
        self.links, self.order, self.sums, self.total = links, order, [], None
        self.pending = None

    def swap(self, mine, other):
        self.mine, self.other = mine, self.links.swap(self.order.gate(other))

    def add(self):
        total = self.mine + self.order.gate(self.other).astype(f32)
        count = max(self.links.chips // 2, 1)
        size = total.shape[0] // count
        self.sums.extend(total[j * size : (j + 1) * size] for j in range(count))

    def send(self):
        send = self.total.astype(bf16)
        self.order.mark(send)
        self.pending = self.links.ring(send)

    def arrive(self):
        self.got = self.order.gate(self.pending)
        self.order.mark(self.got)

    def receive(self, index):
        self.arrive()
        self.total = self.got.astype(f32) + self.sums[index]


VMEM = pl.BlockSpec(memory_space=pltpu.VMEM)
ANY = pl.BlockSpec(memory_space=pl.ANY)
SMEM = pl.BlockSpec(memory_space=pltpu.SMEM)
MIB = 2**20
TOKEN = jax.ShapeDtypeStruct((8, 128), f32)


def params(mib):
    return pltpu.CompilerParams(vmem_limit_bytes=mib * MIB)


def cost(rows, depth, columns, bytes_accessed):
    return pl.CostEstimate(
        flops=2 * rows * depth * columns, bytes_accessed=bytes_accessed, transcendentals=0
    )


def width_of(columns):
    return next(width for width in (512, 384, 256, 128) if columns % width == 0)


def stage(weight, after):
    def kernel(weight_ref, *refs):
        out_ref, token_ref, sem = refs[-3:]
        copy = pltpu.make_async_copy(weight_ref, out_ref, sem)
        copy.start()
        token_ref[...] = jnp.zeros_like(token_ref)
        copy.wait()

    return pl.pallas_call(
        kernel,
        in_specs=[ANY] * (1 + len(after)),
        out_specs=[VMEM, VMEM],
        out_shape=[pltpu.VMEM(weight.shape, weight.dtype), TOKEN],
        scratch_shapes=[pltpu.SemaphoreType.DMA],
        compiler_params=params(2),
        name="stage_weight",
        cost_estimate=pl.CostEstimate(flops=0, bytes_accessed=weight.size * 2, transcendentals=0),
    )(pltpu.with_memory_space_constraint(weight, pltpu.HBM), *after)


class Weight:
    def __init__(self, value, mode, width, last):
        self.value, self.mode, self.width, self.last = value, mode, width, last
        self.count = (value.shape[0] if last else value.shape[1]) // width
        held, kept, read = (mode == name for name in ("held", "kept", "read"))
        self.in_spec = VMEM if held else ANY
        space = pltpu.VMEM if held else pltpu.HBM
        self.operand = pltpu.with_memory_space_constraint(value, space)
        self.out_specs = [VMEM] if kept else []
        self.out_shape = [pltpu.VMEM(value.shape, value.dtype)] if kept else []
        self.scratch = [pltpu.VMEM(value.shape, value.dtype)] if read else []
        self.scratch += [] if held else [pltpu.SemaphoreType.DMA((self.count,))]
        self.limit = 14 + (value.size * 2 // MIB + 1 if read else 0)

    def place(self, weight_ref, outs):
        if self.mode == "held":
            return weight_ref, ()
        staged_ref = outs[4] if self.mode == "kept" else outs[-2]
        return staged_ref, (weight_ref, staged_ref, outs[-1])

    def copy(self, weight_ref, staged_ref, sems, step):
        start = step * self.width if isinstance(step, int) else pl.multiple_of(step * self.width, self.width)
        part = (pl.ds(start, self.width), slice(None))
        part = part if self.last else part[::-1]
        return pltpu.make_async_copy(weight_ref.at[part], staged_ref.at[part], sems.at[step])

    def begin(self, route):
        for step in range(self.count if route else 0):
            self.copy(*route, step).start()

    def wait(self, step, route):
        if route:
            self.copy(*route, step).wait()


def product(left, weight_ref, start, width, last):
    if last:
        return lax.dot_general(
            left, weight_ref[pl.ds(start, width), :], (((1,), (1,)), ((), ())),
            preferred_element_type=f32,
        )
    return jnp.dot(left, weight_ref[:, pl.ds(start, width)], preferred_element_type=f32)


def to_send(links, units, rows, weight, mode, last, after):
    first, size = rows
    depth = units[0].shape[1]
    tokens = size * len(units)
    block = tokens // links.rows
    columns = weight.shape[0] if last else weight.shape[1]
    width = width_of(columns)
    source = Weight(weight, mode, width, last)

    def kernel(*refs):
        unit_refs, weight_ref = refs[: len(units)], refs[len(units)]
        outs = refs[len(units) + 1 + len(after) :]
        left_out, keep_ref, send_ref, token_ref = outs[:4]
        staged_ref, route = source.place(weight_ref, outs)
        left_ref, sem = outs[4 + len(source.out_specs) :][:2]
        source.begin(route)
        for index, unit_ref in enumerate(unit_refs):
            at, within = divmod(index * size, block)
            row = pl.multiple_of(links.position_of(at) * block + within, size)
            left_ref[pl.ds(row, size), :] = unit_ref[first : first + size, :]
        token_ref[...] = jnp.zeros_like(token_ref)
        copy = pltpu.make_async_copy(left_ref, left_out, sem)
        copy.start()

        @pl.loop(0, columns // width)
        def _(step):
            source.wait(step, route)
            start = pl.multiple_of(step * width, width)
            result = product(left_ref[...], staged_ref, start, width, last)
            keep_ref[:, pl.ds(start, width)] = result[: tokens // 2]
            send_ref[:, pl.ds(start, width)] = result[tokens // 2 :].astype(bf16)

        copy.wait()

    half = (tokens // 2, columns)
    left, keep, send, token, *copied = pl.pallas_call(
        kernel,
        in_specs=[VMEM] * len(units) + [source.in_spec] + [ANY] * len(after),
        out_specs=[ANY] + [VMEM] * 3 + source.out_specs,
        out_shape=[
            pltpu.HBM((tokens, depth), bf16),
            jax.ShapeDtypeStruct(half, f32),
            jax.ShapeDtypeStruct(half, bf16),
            TOKEN,
        ]
        + source.out_shape,
        scratch_shapes=[pltpu.VMEM((tokens, depth), bf16), pltpu.SemaphoreType.DMA] + source.scratch,
        compiler_params=params(source.limit),
        name="product_to_send",
        cost_estimate=cost(tokens, depth, columns, 8 * MIB),
    )(*units, source.operand, *after)
    return left, keep, send, (copied + [weight])[0], token


def to_scatter(links, pieces, weight, mode, last, after):
    tokens = sum(piece.shape[0] for piece in pieces)
    block, depth = pieces[0].shape
    size = tokens * 2 // links.cols
    columns = weight.shape[0] if last else weight.shape[1]
    width = width_of(columns)
    source = Weight(weight, mode, width, last)

    def kernel(*refs):
        piece_refs, weight_ref = refs[: len(pieces)], refs[len(pieces)]
        outs = refs[len(pieces) + 1 + len(after) :]
        left_out, mine_ref, other_ref, token_ref = outs[:4]
        staged_ref, route = source.place(weight_ref, outs)
        left_ref, result_ref, sem = outs[4 + len(source.out_specs) :][:3]
        source.begin(route)
        row = 0
        for piece_ref in piece_refs:
            left_ref[row : row + piece_ref.shape[0], :] = piece_ref[...]
            row += piece_ref.shape[0]
        token_ref[...] = jnp.zeros_like(token_ref)
        copy = pltpu.make_async_copy(left_ref, left_out, sem)
        copy.start()

        @pl.loop(0, columns // width)
        def _(step):
            source.wait(step, route)
            start = pl.multiple_of(step * width, width)
            result_ref[...] = product(left_ref[...], staged_ref, start, width, last)
            for unit in range(tokens // size):
                at, within = divmod(unit * size, block)
                row = pl.multiple_of(links.position_of(at) * block + within, size)
                value = result_ref[pl.ds(row, size), :]
                to = slice(unit // 2 * size, (unit // 2 + 1) * size)
                if unit % 2:
                    other_ref[to, pl.ds(start, width)] = value.astype(bf16)
                else:
                    mine_ref[to, pl.ds(start, width)] = value

        copy.wait()

    half = (tokens // 2, columns)
    left, mine, other, token, *copied = pl.pallas_call(
        kernel,
        in_specs=[VMEM] * len(pieces) + [source.in_spec] + [ANY] * len(after),
        out_specs=[ANY] + [VMEM] * 3 + source.out_specs,
        out_shape=[
            pltpu.HBM((tokens, depth), bf16),
            jax.ShapeDtypeStruct(half, f32),
            jax.ShapeDtypeStruct(half, bf16),
            TOKEN,
        ]
        + source.out_shape,
        scratch_shapes=[
            pltpu.VMEM((tokens, depth), bf16),
            pltpu.VMEM((tokens, width), f32),
            pltpu.SemaphoreType.DMA,
        ]
        + source.scratch,
        compiler_params=params(source.limit),
        name="product_to_scatter",
        cost_estimate=cost(tokens, depth, columns, 8 * MIB),
    )(*pieces, source.operand, *after)
    return left, mine, other, (copied + [weight])[0], token


def weight_grad(lefts, rights, part, base, after):
    tokens, rows = lefts[0].shape
    columns = rights[0].shape[1]
    width = width_of(rows // 2)
    steps = rows // 2 // width
    count = len(lefts)

    def kernel(*refs):
        left_refs, right_refs = refs[:count], refs[count : 2 * count]
        out_ref, token_ref = refs[-3], refs[-1]

        @pl.when(pl.program_id(0) == 0)
        def _():
            ones = jnp.ones((16, tokens), bf16)
            total = sum(jnp.dot(ones, ref[...], preferred_element_type=f32) for ref in right_refs)
            refs[-2][...] = total[:8]
            token_ref[...] = jnp.zeros_like(token_ref)

        total = sum(
            lax.dot_general(
                left[...], right[...], (((0,), (0,)), ((), ())), preferred_element_type=f32
            )
            for left, right in zip(left_refs, right_refs)
        )
        out_ref[...] = total.astype(bf16)

    extra = list(after) + ([] if base is None else [base])
    out, sums, token = pl.pallas_call(
        kernel,
        grid=(steps,),
        in_specs=[pl.BlockSpec((tokens, width), lambda i: (0, i + part * steps))] * count
        + [pl.BlockSpec((tokens, columns), lambda i: (0, 0), pipeline_mode=pl.Buffered(1))] * count
        + [ANY] * len(extra),
        out_specs=[
            pl.BlockSpec((width, columns), lambda i: (i + part * steps, 0)),
            pl.BlockSpec((8, columns), lambda i: (0, 0)),
            pl.BlockSpec((8, 128), lambda i: (0, 0)),
        ],
        out_shape=[
            jax.ShapeDtypeStruct((rows, columns), bf16),
            jax.ShapeDtypeStruct((8, columns), f32),
            TOKEN,
        ],
        input_output_aliases={} if base is None else {2 * count + len(after): 0},
        compiler_params=params(24),
        name="weight_grad",
        cost_estimate=cost(rows // 2, count * tokens, columns, rows * columns),
    )(*lefts, *rights, *extra)
    return out, sums[0], token


def per_device(links, inputs, in_weight, in_bias, out_weight, out_bias, cotangent):
    half, chips = max(links.chips // 2, 1), links.chips
    order = Order()
    whole = (0, inputs.shape[0])

    def bring(arrivals, swaps, pending, count):
        for _ in range(count):
            value = order.gate(pending)
            order.mark(value)
            arrivals.append(value)
            pending = links.ring(value) if len(arrivals) < chips else None
            swaps.append(links.swap(value))
        return pending

    def units(arrivals, swapped, part):
        chosen = slice(part * half, (part + 1) * half)
        return [u for pair in zip(arrivals[chosen], swapped[chosen]) for u in pair]

    ins, cots = [inputs], [cotangent]
    next_in, next_cot = links.ring(inputs), links.ring(cotangent)
    in_swaps, cot_swaps = [links.swap(inputs)], [links.swap(cotangent)]
    (staged,) = order.run(stage, in_weight)
    next_in = bring(ins, in_swaps, next_in, half - 1)
    left_in0, keep, send, _ = order.run(
        to_send, links, units(ins, in_swaps, 0), whole, staged, "held", False
    )
    sum_p0 = RowSum(links, order, keep, send)
    next_cot = bring(cots, cot_swaps, next_cot, half - 1)
    left_cot0, keep, send, _ = order.run(
        to_send, links, units(cots, cot_swaps, 0), whole, out_weight, "read", True
    )
    sum_g0 = RowSum(links, order, keep, send)
    sum_p0.middle()
    next_in = bring(ins, in_swaps, next_in, half - 1)
    hidden, slope0 = gelu_both(sum_p0.finish() + in_bias)
    hid0 = RowGather(links, order, hidden.astype(bf16))
    sum_g0.middle()
    next_cot = bring(cots, cot_swaps, next_cot, half - 1)
    hid0.middle()
    bring(ins, in_swaps, next_in, 1)
    left_in1, keep, send, _ = order.run(
        to_send, links, units(ins, in_swaps, 1), whole, in_weight, "read", False
    )
    sum_p1 = RowSum(links, order, keep, send)
    grad0 = RowGather(links, order, (sum_g0.finish() * slope0).astype(bf16))
    bring(cots, cot_swaps, next_cot, 1)
    grad0.middle()
    left_cot1, keep, send, staged = order.run(
        to_send, links, units(cots, cot_swaps, 1), whole, out_weight, "kept", True
    )
    sum_g1 = RowSum(links, order, keep, send)
    sum_p1.middle()
    left_hid0, mine, other, _ = order.run(to_scatter, links, hid0.finish(), staged, "held", False)
    hidden, slope1 = gelu_both(sum_p1.finish() + in_bias)
    hid1 = RowGather(links, order, hidden.astype(bf16))
    outs = ChipSum(links, order)
    outs.swap(mine, other)
    grads0 = grad0.finish()
    order.mark(grads0[-1])
    left_grad0, mine, other, _ = order.run(to_scatter, links, grads0, in_weight, "read", True)
    hid1.middle()
    sum_g1.middle()
    outs.add()
    outs.total = outs.sums[1]
    for index in range(2, half):
        outs.send()
        outs.receive(index)
    outs.send()
    igs = ChipSum(links, order)
    igs.swap(mine, other)
    grad1 = RowGather(links, order, (sum_g1.finish() * slope1).astype(bf16))
    left_hid1, mine, other, _ = order.run(to_scatter, links, hid1.finish(), staged, "held", False)
    grad1.middle()
    outs.arrive()
    outs.swap(mine, other)
    igs.add()
    igs.total = igs.sums[1]
    for index in range(2, half):
        igs.send()
        igs.receive(index)
    igs.send()
    hids, cot_lefts = [left_hid0, left_hid1], [left_cot0, left_cot1]
    partial, out_bias_grad = order.run(weight_grad, hids, cot_lefts, 0, None)
    grads1 = grad1.finish()
    order.mark(grads1[-1])
    outs.add()
    outs.total = outs.got.astype(f32) + outs.sums[half]
    outs.send()
    left_grad1, mine, other, _ = order.run(to_scatter, links, grads1, in_weight, "read", True)
    igs.arrive()
    igs.swap(mine, other)
    for index in range(half + 1, chips):
        outs.receive(index)
        outs.send()
    igs.add()
    igs.total = igs.got.astype(f32) + igs.sums[half]
    igs.send()
    out_weight_grad, _ = order.run(weight_grad, hids, cot_lefts, 1, partial)
    outs.receive(0)
    in_lefts, grads = [left_in0, left_in1], [left_grad0, left_grad1]
    partial, in_bias_grad = order.run(weight_grad, in_lefts, grads, 0, None)
    for index in range(half + 1, chips):
        igs.receive(index)
        igs.send()
    in_weight_grad, _ = order.run(weight_grad, in_lefts, grads, 1, partial)
    igs.receive(0)

    output = (outs.total + out_bias).astype(bf16)
    input_grad = igs.total.astype(bf16)
    return (output, input_grad, in_weight_grad, out_weight_grad, in_bias_grad, out_bias_grad)


def solution(mesh):
    links = Links(mesh.shape["row"], mesh.shape["col"])
    in_specs = (
        P("col", "row"),
        P("row", "col"),
        P("col"),
        P("col", "row"),
        P("row"),
        P("col", "row"),
    )
    out_specs = (
        P("col", "row"),
        P("col", "row"),
        P("row", "col"),
        P("col", "row"),
        P("col"),
        P("row"),
    )

    def step(*arrays):
        return per_device(links, *arrays)

    return jax.shard_map(
        step, mesh=mesh, in_specs=in_specs, out_specs=out_specs, check_vma=False
    )
```

profile of v0, /device:TPU:0, one launch (start us, length us, event | category | flops | bytes accessed | tf_op | source)
XLA Modules:
  0.0 201.4 jit_solution(7251434021714773977)
XLA Ops:
  0.7 4.1 %collective-permute-start.1 = (bf16[64,3072]{1,0:T(8,128)(2,1)}, bf16[64,3072]{1,0:T(8,128)(2,1)S(1)}, u32[]{:S(2)}, u32[]{:S(2)}) collective-permute-start(bf16[64,3072]{1,0:T(8,128)(2,1)} %refs_0_.2), channel_id=1, source_target_pairs={{0,4},{1,5},{4,6},{5,7},{6,2},{7,3},{2,0},{3,1},{8,12},{9,13},{12,... | collective-permute-start | bytes 1179656 | tf_op jit(solution)/shard_map/ppermute | solution.py:40
  4.7 6.4 %stage_weight.1 = (bf16[3072,3072]{1,0:T(8,128)(2,1)S(1)}, f32[8,128]{1,0:T(8,128)S(1)}) custom-call(bf16[3072,3072]{1,0:T(8,128)(2,1)} %refs_3_.3), custom_call_target="tpu_custom_call" | custom-call | bytes 18874368 | tf_op jit(solution)/shard_map/stage_weight/pallas_call | solution.py:202
  13.9 3.3 %collective-permute-start.5 = (bf16[64,3072]{1,0:T(8,128)(2,1)S(1)}, bf16[64,3072]{1,0:T(8,128)(2,1)S(1)}, u32[]{:S(2)}, u32[]{:S(2)}) collective-permute-start(bf16[64,3072]{1,0:T(8,128)(2,1)S(1)} %copy-done.9), channel_id=1, source_target_pairs={{0,4},{1,5},{4,6},{5,7},{6,2},{7,3},{2,0},{3,1},{8,12},{9,13},{12,... | collective-permute-start | bytes 1179656 | tf_op jit(solution)/shard_map/ppermute | solution.py:40
  17.2 6.1 %product_to_send.4 = (bf16[256,3072]{1,0:T(8,128)(2,1)}, f32[128,3072]{1,0:T(8,128)S(1)}, bf16[128,3072]{1,0:T(8,128)(2,1)S(1)}, f32[8,128]{1,0:T(8,128)S(1)}) custom-call(bf16[64,3072]{1,0:T(8,128)(2,1)S(1)} %copy-done.8, bf16[64,3072]{1,0:T(8,128)(2,1)S(1)} %collective-permute-done.refs_1_, bf16[64,3072]{1,0:T(8,128)(2,1)S(1)} %collective-permute-done.1.refs_2_, ...), custom_call_target="tpu_custom_call" | custom-call | flops 4831838208 | bytes 8388608 | tf_op jit(solution)/shard_map/product_to_send/pallas_call | solution.py:293
  23.3 2.4 %collective-permute-done.5.refs_2_ = bf16[64,3072]{1,0:T(8,128)(2,1)S(1)} collective-permute-done((bf16[64,3072]{1,0:T(8,128)(2,1)S(1)}, bf16[64,3072]{1,0:T(8,128)(2,1)S(1)}, u32[]{:S(2)}, u32[]{:S(2)}) %collective-permute-start.5) | collective-permute-done | bytes 393248 | tf_op jit(solution)/shard_map/ppermute | solution.py:40
  27.3 3.4 %collective-permute-start.8 = (bf16[64,3072]{1,0:T(8,128)(2,1)S(1)}, bf16[64,3072]{1,0:T(8,128)(2,1)S(1)}, u32[]{:S(2)}, u32[]{:S(2)}) collective-permute-start(bf16[64,3072]{1,0:T(8,128)(2,1)S(1)} %collective-permute-done.1.refs_2_), channel_id=1, source_target_pairs={{0,4},{1,5},{4,6},{5,7},{6,2},{7,3},{2,0},{3,1},{8,12},{9,13},{12,... | collective-permute-start | bytes 1179656 | tf_op jit(solution)/shard_map/ppermute | solution.py:40
  30.6 8.6 %product_to_send.5 = (bf16[256,3072]{1,0:T(8,128)(2,1)}, f32[128,3072]{1,0:T(8,128)S(1)}, bf16[128,3072]{1,0:T(8,128)(2,1)S(1)}, f32[8,128]{1,0:T(8,128)S(1)}) custom-call(bf16[64,3072]{1,0:T(8,128)(2,1)S(1)} %copy-done.9, bf16[64,3072]{1,0:T(8,128)(2,1)S(1)} %collective-permute-done.4.refs_1_, bf16[64,3072]{1,0:T(8,128)(2,1)S(1)} %collective-permute-done.5.refs_2_, ...), custom_call_target="tpu_custom_call" | custom-call | flops 4831838208 | bytes 8388608 | tf_op jit(solution)/shard_map/product_to_send/pallas_call | solution.py:293
  41.6 2.8 %collective-permute-start.11 = (bf16[64,3072]{1,0:T(8,128)(2,1)S(1)}, bf16[64,3072]{1,0:T(8,128)(2,1)S(1)}, u32[]{:S(2)}, u32[]{:S(2)}) collective-permute-start(bf16[64,3072]{1,0:T(8,128)(2,1)S(1)} %collective-permute-done.5.refs_2_), channel_id=1, source_target_pairs={{0,4},{1,5},{4,6},{5,7},{6,2},{7,3},{2,0},{3,1},{8,12},{9,13},{12,... | collective-permute-start | bytes 1179656 | tf_op jit(solution)/shard_map/ppermute | solution.py:40
  44.5 6.8 %collective-permute-done.7 = bf16[64,3072]{1,0:T(8,128)(2,1)S(1)} collective-permute-done((bf16[64,3072]{1,0:T(8,128)(2,1)S(1)}, bf16[64,3072]{1,0:T(8,128)(2,1)S(1)}, u32[]{:S(2)}, u32[]{:S(2)}) %collective-permute-start.7) | collective-permute-done | bytes 393248 | tf_op jit(solution)/shard_map/ppermute | solution.py:51
  53.4 4.3 %collective-permute-done.10 = bf16[128,3072]{1,0:T(8,128)(2,1)S(1)} collective-permute-done((bf16[128,3072]{1,0:T(8,128)(2,1)S(1)}, bf16[128,3072]{1,0:T(8,128)(2,1)S(1)}, u32[]{:S(2)}, u32[]{:S(2)}) %collective-permute-start.10) | collective-permute-done | bytes 786464 | tf_op jit(solution)/shard_map/ppermute | solution.py:51
  60.9 3.0 %collective-permute-start.14 = (bf16[64,3072]{1,0:T(8,128)(2,1)S(1)}, bf16[64,3072]{1,0:T(8,128)(2,1)S(1)}, u32[]{:S(2)}, u32[]{:S(2)}) collective-permute-start(bf16[64,3072]{1,0:T(8,128)(2,1)S(1)} %collective-permute-done.11.refs_0_), channel_id=1, source_target_pairs={{0,4},{1,5},{4,6},{5,7},{6,2},{7,3},{2,0},{3,1},{8,12},{9,13},{12,... | collective-permute-start | bytes 1179656 | tf_op jit(solution)/shard_map/ppermute | solution.py:40
  64.4 8.5 %product_to_send.6 = (bf16[256,3072]{1,0:T(8,128)(2,1)}, f32[128,3072]{1,0:T(8,128)S(1)}, bf16[128,3072]{1,0:T(8,128)(2,1)S(1)}, f32[8,128]{1,0:T(8,128)S(1)}) custom-call(bf16[64,3072]{1,0:T(8,128)(2,1)S(1)} %collective-permute-done.8.refs_0_, bf16[64,3072]{1,0:T(8,128)(2,1)S(1)} %collective-permute-done.15.refs_1_, ...), custom_call_target="tpu_custom_call" | custom-call | flops 4831838208 | bytes 8388608 | tf_op jit(solution)/shard_map/product_to_send/pallas_call | solution.py:293
  77.6 6.7 %collective-permute-done.20.refs_1_ = bf16[64,3072]{1,0:T(8,128)(2,1)S(1)} collective-permute-done((bf16[64,3072]{1,0:T(8,128)(2,1)S(1)}, bf16[64,3072]{1,0:T(8,128)(2,1)S(1)}, u32[]{:S(2)}, u32[]{:S(2)}) %collective-permute-start.20) | collective-permute-done | bytes 393248 | tf_op jit(solution)/shard_map/ppermute | solution.py:51
  86.2 8.6 %product_to_send.7 = (bf16[256,3072]{1,0:T(8,128)(2,1)}, f32[128,3072]{1,0:T(8,128)S(1)}, bf16[128,3072]{1,0:T(8,128)(2,1)S(1)}, f32[8,128]{1,0:T(8,128)S(1)}, bf16[3072,3072]{1,0:T(8,128)(2,1)S(1)}) custom-call(bf16[64,3072]{1,0:T(8,128)(2,1)S(1)} %collective-permute-done.11.refs_0_, bf16[64,3072]{1,0:T(8,128)(2,1)S(1)} %collective-permute-done.13.refs_1_, ...), custom_call_target="tpu_custom_call" | custom-call | flops 4831838208 | bytes 8388608 | tf_op jit(solution)/shard_map/product_to_send/pallas_call | solution.py:293
  98.6 6.3 %product_to_scatter.4 = (bf16[256,3072]{1,0:T(8,128)(2,1)}, f32[128,3072]{1,0:T(8,128)S(1)}, bf16[128,3072]{1,0:T(8,128)(2,1)S(1)}, f32[8,128]{1,0:T(8,128)S(1)}) custom-call(bf16[64,3072]{1,0:T(8,128)(2,1)S(1)} %multiply_convert_fusion.1.refs_0_, bf16[64,3072]{1,0:T(8,128)(2,1)S(1)} %collective-permute-done.9.refs_1_, ...), custom_call_target="tpu_custom_call" | custom-call | flops 4831838208 | bytes 8388608 | tf_op jit(solution)/shard_map/product_to_scatter/pallas_call | solution.py:353
  105.0 4.6 %collective-permute-done.22 = bf16[64,3072]{1,0:T(8,128)(2,1)S(1)} collective-permute-done((bf16[64,3072]{1,0:T(8,128)(2,1)S(1)}, bf16[64,3072]{1,0:T(8,128)(2,1)S(1)}, u32[]{:S(2)}, u32[]{:S(2)}) %collective-permute-start.22) | collective-permute-done | bytes 393248 | tf_op jit(solution)/shard_map/ppermute | solution.py:51
  111.1 8.9 %product_to_scatter.5 = (bf16[256,3072]{1,0:T(8,128)(2,1)}, f32[128,3072]{1,0:T(8,128)S(1)}, bf16[128,3072]{1,0:T(8,128)(2,1)S(1)}, f32[8,128]{1,0:T(8,128)S(1)}) custom-call(bf16[64,3072]{1,0:T(8,128)(2,1)S(1)} %fusion.6.refs_0_, bf16[64,3072]{1,0:T(8,128)(2,1)S(1)} %collective-permute-done.20.refs_1_, ...), custom_call_target="tpu_custom_call" | custom-call | flops 4831838208 | bytes 8388608 | tf_op jit(solution)/shard_map/product_to_scatter/pallas_call | solution.py:353
  127.9 8.0 %collective-permute-done.29 = bf16[64,3072]{1,0:T(8,128)(2,1)S(1)} collective-permute-done((bf16[64,3072]{1,0:T(8,128)(2,1)S(1)}, bf16[64,3072]{1,0:T(8,128)(2,1)S(1)}, u32[]{:S(2)}, u32[]{:S(2)}) %collective-permute-start.29) | collective-permute-done | bytes 393248 | tf_op jit(solution)/shard_map/ppermute | solution.py:51
  138.7 6.3 %product_to_scatter.6 = (bf16[256,3072]{1,0:T(8,128)(2,1)}, f32[128,3072]{1,0:T(8,128)S(1)}, bf16[128,3072]{1,0:T(8,128)(2,1)S(1)}, f32[8,128]{1,0:T(8,128)S(1)}) custom-call(bf16[64,3072]{1,0:T(8,128)(2,1)S(1)} %multiply_convert_fusion.refs_0_, bf16[64,3072]{1,0:T(8,128)(2,1)S(1)} %collective-permute-done.25.refs_1_, ...), custom_call_target="tpu_custom_call" | custom-call | flops 4831838208 | bytes 8388608 | tf_op jit(solution)/shard_map/product_to_scatter/pallas_call | solution.py:353
  149.3 7.8 %weight_grad.4 = (bf16[3072,3072]{1,0:T(8,128)(2,1)}, f32[8,3072]{1,0:T(8,128)S(1)}, f32[8,128]{1,0:T(8,128)S(1)}) custom-call(bf16[256,3072]{1,0:T(8,128)(2,1)S(1)} %copy-done.5, bf16[256,3072]{1,0:T(8,128)(2,1)S(1)} %copy-done.6, bf16[256,3072]{1,0:T(8,128)(2,1)S(1)} %copy-done.1, bf16[256,3072]{1,0:T(8,128)(2,1)S(1)} %copy-done.3, ...), custom_call_target="tpu_custom_call" | custom-call | flops 4831838208 | bytes 9437184 | tf_op jit(solution)/shard_map/weight_grad/pallas_call | solution.py:404
  158.9 8.9 %product_to_scatter.7 = (bf16[256,3072]{1,0:T(8,128)(2,1)}, f32[128,3072]{1,0:T(8,128)S(1)}, bf16[128,3072]{1,0:T(8,128)(2,1)S(1)}, f32[8,128]{1,0:T(8,128)S(1)}) custom-call(bf16[64,3072]{1,0:T(8,128)(2,1)S(1)} %fusion.13.refs_0_, bf16[64,3072]{1,0:T(8,128)(2,1)S(1)} %collective-permute-done.30.refs_1_, ...), custom_call_target="tpu_custom_call" | custom-call | flops 4831838208 | bytes 8388608 | tf_op jit(solution)/shard_map/product_to_scatter/pallas_call | solution.py:353
  171.3 7.8 %weight_grad.5 = (bf16[3072,3072]{1,0:T(8,128)(2,1)}, f32[8,3072]{1,0:T(8,128)}, f32[8,128]{1,0:T(8,128)S(1)}) custom-call(bf16[256,3072]{1,0:T(8,128)(2,1)S(1)} %copy-done.5, bf16[256,3072]{1,0:T(8,128)(2,1)S(1)} %copy-done.6, bf16[256,3072]{1,0:T(8,128)(2,1)S(1)} %copy-done.1, bf16[256,3072]{1,0:T(8,128)(2,1)S(1)} %copy-done.3, ...), custom_call_target="tpu_custom_call", output_to_operand_aliasing={{0}: (5, {})} | custom-call | flops 4831838208 | bytes 9437184 | tf_op jit(solution)/shard_map/weight_grad/pallas_call | solution.py:404
  181.1 7.8 %weight_grad.6 = (bf16[3072,3072]{1,0:T(8,128)(2,1)}, f32[8,3072]{1,0:T(8,128)S(1)}, f32[8,128]{1,0:T(8,128)S(1)}) custom-call(bf16[256,3072]{1,0:T(8,128)(2,1)S(1)} %copy-done, bf16[256,3072]{1,0:T(8,128)(2,1)S(1)} %copy-done.2, bf16[256,3072]{1,0:T(8,128)(2,1)S(1)} %copy-done.4, bf16[256,3072]{1,0:T(8,128)(2,1)S(1)} %copy-done.7, ...), custom_call_target="tpu_custom_call" | custom-call | flops 4831838208 | bytes 9437184 | tf_op jit(solution)/shard_map/weight_grad/pallas_call | solution.py:404
  192.7 7.8 %weight_grad.7 = (bf16[3072,3072]{1,0:T(8,128)(2,1)}, f32[8,3072]{1,0:T(8,128)}, f32[8,128]{1,0:T(8,128)}) custom-call(bf16[256,3072]{1,0:T(8,128)(2,1)S(1)} %copy-done, bf16[256,3072]{1,0:T(8,128)(2,1)S(1)} %copy-done.2, bf16[256,3072]{1,0:T(8,128)(2,1)S(1)} %copy-done.4, bf16[256,3072]{1,0:T(8,128)(2,1)S(1)} %copy-done.7, ...), custom_call_target="tpu_custom_call", output_to_operand_aliasing={{0}: (5, {})} | custom-call | flops 4831838208 | bytes 9437184 | tf_op jit(solution)/shard_map/weight_grad/pallas_call | solution.py:404
  (125 shorter events, 51.1 us)
Async XLA Ops:
  0.7 12.8 %collective-permute-start.1 = (bf16[64,3072]{1,0:T(8,128)(2,1)}, bf16[64,3072]{1,0:T(8,128)(2,1)S(1)}, u32[]{:S(2)}, u32[]{:S(2)}) collective-permute-start(bf16[64,3072]{1,0:T(8,128)(2,1)} %refs_0_.2), channel_id=1, source_target_pairs={{0,4},{1,5},{4,6},{5,7},{6,2},{7,3},{2,0},{3,1},{8,12},{9,13},{12,... | collective-permute-start | bytes 1179656 | tf_op jit(solution)/shard_map/ppermute | solution.py:40
  4.7 12.5 %collective-permute-start = (bf16[64,3072]{1,0:T(8,128)(2,1)}, bf16[64,3072]{1,0:T(8,128)(2,1)S(1)}, u32[]{:S(2)}, u32[]{:S(2)}) collective-permute-start(bf16[64,3072]{1,0:T(8,128)(2,1)} %refs_0_.2), channel_id=1, source_target_pairs={{0,1},{1,0},{2,3},{3,2},{4,5},{5,4},{6,7},{7,6},{8,9},{9,8},{10,11... | collective-permute-start | bytes 1179656 | tf_op jit(solution)/shard_map/ppermute | solution.py:43
  13.4 17.2 %collective-permute-start.4 = (bf16[64,3072]{1,0:T(8,128)(2,1)S(1)}, bf16[64,3072]{1,0:T(8,128)(2,1)S(1)}, u32[]{:S(2)}, u32[]{:S(2)}) collective-permute-start(bf16[64,3072]{1,0:T(8,128)(2,1)S(1)} %copy-done.9), channel_id=1, source_target_pairs={{0,1},{1,0},{2,3},{3,2},{4,5},{5,4},{6,7},{7,6},{8,9},{9,8},{10,11... | collective-permute-start | bytes 1179656 | tf_op jit(solution)/shard_map/ppermute | solution.py:43
  25.8 13.5 %collective-permute-start.3 = (bf16[128,3072]{1,0:T(8,128)(2,1)S(1)}, bf16[128,3072]{1,0:T(8,128)(2,1)S(1)}, u32[]{:S(2)}, u32[]{:S(2)}) collective-permute-start(bf16[128,3072]{1,0:T(8,128)(2,1)S(1)} %get-tuple-element.121), channel_id=1, source_target_pairs={{0,8},{1,17},{2,10},{3,19},{4,12},{5,21},{6,14},{7,23},{8,0},{9,25... | collective-permute-start | bytes 2359304 | tf_op jit(solution)/shard_map/ppermute | solution.py:51
  27.3 17.2 %collective-permute-start.8 = (bf16[64,3072]{1,0:T(8,128)(2,1)S(1)}, bf16[64,3072]{1,0:T(8,128)(2,1)S(1)}, u32[]{:S(2)}, u32[]{:S(2)}) collective-permute-start(bf16[64,3072]{1,0:T(8,128)(2,1)S(1)} %collective-permute-done.1.refs_2_), channel_id=1, source_target_pairs={{0,4},{1,5},{4,6},{5,7},{6,2},{7,3},{2,0},{3,1},{8,12},{9,13},{12,... | collective-permute-start | bytes 1179656 | tf_op jit(solution)/shard_map/ppermute | solution.py:40
  41.1 16.6 %collective-permute-start.10 = (bf16[128,3072]{1,0:T(8,128)(2,1)S(1)}, bf16[128,3072]{1,0:T(8,128)(2,1)S(1)}, u32[]{:S(2)}, u32[]{:S(2)}) collective-permute-start(bf16[128,3072]{1,0:T(8,128)(2,1)S(1)} %get-tuple-element.133), channel_id=1, source_target_pairs={{0,8},{1,17},{2,10},{3,19},{4,12},{5,21},{6,14},{7,23},{8,0},{9,25... | collective-permute-start | bytes 2359304 | tf_op jit(solution)/shard_map/ppermute | solution.py:51
  41.6 16.3 %collective-permute-start.11 = (bf16[64,3072]{1,0:T(8,128)(2,1)S(1)}, bf16[64,3072]{1,0:T(8,128)(2,1)S(1)}, u32[]{:S(2)}, u32[]{:S(2)}) collective-permute-start(bf16[64,3072]{1,0:T(8,128)(2,1)S(1)} %collective-permute-done.5.refs_2_), channel_id=1, source_target_pairs={{0,4},{1,5},{4,6},{5,7},{6,2},{7,3},{2,0},{3,1},{8,12},{9,13},{12,... | collective-permute-start | bytes 1179656 | tf_op jit(solution)/shard_map/ppermute | solution.py:40
  44.4 19.9 %collective-permute-start.15 = (bf16[64,3072]{1,0:T(8,128)(2,1)S(1)}, bf16[64,3072]{1,0:T(8,128)(2,1)S(1)}, u32[]{:S(2)}, u32[]{:S(2)}) collective-permute-start(bf16[64,3072]{1,0:T(8,128)(2,1)S(1)} %collective-permute-done.8.refs_0_), channel_id=1, source_target_pairs={{0,1},{1,0},{2,3},{3,2},{4,5},{5,4},{6,7},{7,6},{8,9},{9,8},{10,11... | collective-permute-start | bytes 1179656 | tf_op jit(solution)/shard_map/ppermute | solution.py:43
  44.4 16.5 %collective-permute-start.16 = (bf16[64,3072]{1,0:T(8,128)(2,1)S(1)}, bf16[64,3072]{1,0:T(8,128)(2,1)S(1)}, u32[]{:S(2)}, u32[]{:S(2)}) collective-permute-start(bf16[64,3072]{1,0:T(8,128)(2,1)S(1)} %collective-permute-done.8.refs_0_), channel_id=1, source_target_pairs={{0,4},{1,5},{4,6},{5,7},{6,2},{7,3},{2,0},{3,1},{8,12},{9,13},{12,... | collective-permute-start | bytes 1179656 | tf_op jit(solution)/shard_map/ppermute | solution.py:40
  60.9 14.2 %collective-permute-start.14 = (bf16[64,3072]{1,0:T(8,128)(2,1)S(1)}, bf16[64,3072]{1,0:T(8,128)(2,1)S(1)}, u32[]{:S(2)}, u32[]{:S(2)}) collective-permute-start(bf16[64,3072]{1,0:T(8,128)(2,1)S(1)} %collective-permute-done.11.refs_0_), channel_id=1, source_target_pairs={{0,4},{1,5},{4,6},{5,7},{6,2},{7,3},{2,0},{3,1},{8,12},{9,13},{12,... | collective-permute-start | bytes 1179656 | tf_op jit(solution)/shard_map/ppermute | solution.py:40
  75.6 23.0 %collective-permute-start.12 = (bf16[128,3072]{1,0:T(8,128)(2,1)}, bf16[128,3072]{1,0:T(8,128)(2,1)S(1)}, u32[]{:S(2)}, u32[]{:S(2)}) collective-permute-start(bf16[128,3072]{1,0:T(8,128)(2,1)} %pad_maximum_fusion), channel_id=1, source_target_pairs={{0,8},{1,17},{2,10},{3,19},{4,12},{5,21},{6,14},{7,23},{8,0},{9,25... | collective-permute-start | bytes 2359304 | tf_op jit(solution)/shard_map/ppermute | solution.py:51
  76.1 21.1 %collective-permute-start.21 = (bf16[128,3072]{1,0:T(8,128)(2,1)S(1)}, bf16[128,3072]{1,0:T(8,128)(2,1)S(1)}, u32[]{:S(2)}, u32[]{:S(2)}) collective-permute-start(bf16[128,3072]{1,0:T(8,128)(2,1)S(1)} %get-tuple-element.151), channel_id=1, source_target_pairs={{0,8},{1,17},{2,10},{3,19},{4,12},{5,21},{6,14},{7,23},{8,0},{9,25... | collective-permute-start | bytes 2359304 | tf_op jit(solution)/shard_map/ppermute | solution.py:51
  84.4 26.7 %collective-permute-start.24 = (bf16[128,3072]{1,0:T(8,128)(2,1)S(1)}, bf16[128,3072]{1,0:T(8,128)(2,1)S(1)}, u32[]{:S(2)}, u32[]{:S(2)}) collective-permute-start(bf16[128,3072]{1,0:T(8,128)(2,1)S(1)} %pad_maximum_fusion.1), channel_id=1, source_target_pairs={{0,8},{1,17},{2,10},{3,19},{4,12},{5,21},{6,14},{7,23},{8,0},{9,25... | collective-permute-start | bytes 2359304 | tf_op jit(solution)/shard_map/ppermute | solution.py:51
  94.8 28.8 %collective-permute-start.26 = (bf16[128,3072]{1,0:T(8,128)(2,1)S(1)}, bf16[128,3072]{1,0:T(8,128)(2,1)S(1)}, u32[]{:S(2)}, u32[]{:S(2)}) collective-permute-start(bf16[128,3072]{1,0:T(8,128)(2,1)S(1)} %get-tuple-element.168), channel_id=1, source_target_pairs={{0,8},{1,17},{2,10},{3,19},{4,12},{5,21},{6,14},{7,23},{8,0},{9,25... | collective-permute-start | bytes 2359304 | tf_op jit(solution)/shard_map/ppermute | solution.py:51
  97.4 12.1 %collective-permute-start.22 = (bf16[64,3072]{1,0:T(8,128)(2,1)S(1)}, bf16[64,3072]{1,0:T(8,128)(2,1)S(1)}, u32[]{:S(2)}, u32[]{:S(2)}) collective-permute-start(bf16[64,3072]{1,0:T(8,128)(2,1)S(1)} %slice.143), channel_id=1, source_target_pairs={{0,16},{1,9},{2,18},{3,11},{4,20},{5,13},{6,22},{7,15},{8,24},{9,1... | collective-permute-start | bytes 1179656 | tf_op jit(solution)/shard_map/ppermute | solution.py:51
  109.9 12.1 %collective-permute-start.25 = (bf16[64,3072]{1,0:T(8,128)(2,1)S(1)}, bf16[64,3072]{1,0:T(8,128)(2,1)S(1)}, u32[]{:S(2)}, u32[]{:S(2)}) collective-permute-start(bf16[64,3072]{1,0:T(8,128)(2,1)S(1)} %multiply_convert_fusion.refs_0_), channel_id=1, source_target_pairs={{0,16},{1,9},{2,18},{3,11},{4,20},{5,13},{6,22},{7,15},{8,24},{9,1... | collective-permute-start | bytes 1179656 | tf_op jit(solution)/shard_map/ppermute | solution.py:51
  111.1 13.3 %collective-permute-start.23 = (bf16[128,3072]{1,0:T(8,128)(2,1)S(1)}, bf16[128,3072]{1,0:T(8,128)(2,1)S(1)}, u32[]{:S(2)}, u32[]{:S(2)}) collective-permute-start(bf16[128,3072]{1,0:T(8,128)(2,1)S(1)} %get-tuple-element.161), channel_id=1, source_target_pairs={{0,1},{1,0},{2,3},{3,2},{4,5},{5,4},{6,7},{7,6},{8,9},{9,8},{10,11... | collective-permute-start | bytes 2359304 | tf_op jit(solution)/shard_map/ppermute | solution.py:43
  122.1 16.6 %collective-permute-start.28 = (bf16[128,3072]{1,0:T(8,128)(2,1)S(1)}, bf16[128,3072]{1,0:T(8,128)(2,1)S(1)}, u32[]{:S(2)}, u32[]{:S(2)}) collective-permute-start(bf16[128,3072]{1,0:T(8,128)(2,1)S(1)} %pad_maximum_fusion.2), channel_id=1, source_target_pairs={{0,8},{1,17},{2,10},{3,19},{4,12},{5,21},{6,14},{7,23},{8,0},{9,25... | collective-permute-start | bytes 2359304 | tf_op jit(solution)/shard_map/ppermute | solution.py:51
  123.8 12.1 %collective-permute-start.29 = (bf16[64,3072]{1,0:T(8,128)(2,1)S(1)}, bf16[64,3072]{1,0:T(8,128)(2,1)S(1)}, u32[]{:S(2)}, u32[]{:S(2)}) collective-permute-start(bf16[64,3072]{1,0:T(8,128)(2,1)S(1)} %slice.142), channel_id=1, source_target_pairs={{0,16},{1,9},{2,18},{3,11},{4,20},{5,13},{6,22},{7,15},{8,24},{9,1... | collective-permute-start | bytes 1179656 | tf_op jit(solution)/shard_map/ppermute | solution.py:51
  126.7 20.3 %collective-permute-start.27 = (bf16[64,3072]{1,0:T(8,128)(2,1)S(1)}, bf16[64,3072]{1,0:T(8,128)(2,1)S(1)}, u32[]{:S(2)}, u32[]{:S(2)}) collective-permute-start(bf16[64,3072]{1,0:T(8,128)(2,1)S(1)} %slice.141), channel_id=1, source_target_pairs={{0,4},{1,5},{4,6},{5,7},{6,2},{7,3},{2,0},{3,1},{8,12},{9,13},{12,... | collective-permute-start | bytes 1179656 | tf_op jit(solution)/shard_map/ppermute | solution.py:40
  127.9 19.0 %collective-permute-start.32 = (bf16[128,3072]{1,0:T(8,128)(2,1)S(1)}, bf16[128,3072]{1,0:T(8,128)(2,1)S(1)}, u32[]{:S(2)}, u32[]{:S(2)}) collective-permute-start(bf16[128,3072]{1,0:T(8,128)(2,1)S(1)} %get-tuple-element.190), channel_id=1, source_target_pairs={{0,1},{1,0},{2,3},{3,2},{4,5},{5,4},{6,7},{7,6},{8,9},{9,8},{10,11... | collective-permute-start | bytes 2359304 | tf_op jit(solution)/shard_map/ppermute | solution.py:43
  145.1 12.1 %collective-permute-start.33 = (bf16[128,3072]{1,0:T(8,128)(2,1)S(1)}, bf16[128,3072]{1,0:T(8,128)(2,1)S(1)}, u32[]{:S(2)}, u32[]{:S(2)}) collective-permute-start(bf16[128,3072]{1,0:T(8,128)(2,1)S(1)} %pad_maximum_fusion.3), channel_id=1, source_target_pairs={{0,8},{1,17},{2,10},{3,19},{4,12},{5,21},{6,14},{7,23},{8,0},{9,25... | collective-permute-start | bytes 2359304 | tf_op jit(solution)/shard_map/ppermute | solution.py:51
  147.2 20.6 %collective-permute-start.35 = (bf16[64,3072]{1,0:T(8,128)(2,1)S(1)}, bf16[64,3072]{1,0:T(8,128)(2,1)S(1)}, u32[]{:S(2)}, u32[]{:S(2)}) collective-permute-start(bf16[64,3072]{1,0:T(8,128)(2,1)S(1)} %slice.140), channel_id=1, source_target_pairs={{0,4},{1,5},{4,6},{5,7},{6,2},{7,3},{2,0},{3,1},{8,12},{9,13},{12,... | collective-permute-start | bytes 1179656 | tf_op jit(solution)/shard_map/ppermute | solution.py:40
  170.5 19.9 %collective-permute-start.38 = (bf16[64,3072]{1,0:T(8,128)(2,1)S(1)}, bf16[64,3072]{1,0:T(8,128)(2,1)S(1)}, u32[]{:S(2)}, u32[]{:S(2)}) collective-permute-start(bf16[64,3072]{1,0:T(8,128)(2,1)S(1)} %fusion.18), channel_id=1, source_target_pairs={{0,4},{1,5},{4,6},{5,7},{6,2},{7,3},{2,0},{3,1},{8,12},{9,13},{12,... | collective-permute-start | bytes 1179656 | tf_op jit(solution)/shard_map/ppermute | solution.py:40
  (29 other events, 238.8 us)
where the time goes:
time: 202 us; the launch traced here: 201 us
  Pallas kernels  99.8 us (49%)
  waiting for transfers between devices  45.2 us (22%)
  starting transfers between devices  43.6 us (22%)
  other arithmetic  7.52 us (4%)
  local copies, waits for them, and re-layouts  4.21 us (2%)
    ppermute x16, waiting for transfers between devices, exchange(): return lax.ppermute(value, ('row', 'col'), pairs)  38 us
    pallas_call x4, Pallas kernels, to_send(): pl.pallas_call(kernel, in_specs=[VMEM] * len(units) + [source.in_spec] +...  31.7 us
    pallas_call x4, Pallas kernels, weight_grad(): pl.pallas_call(kernel, grid=(steps,), in_specs=[pl.BlockSpec((tokens, wid...  31.3 us
    pallas_call x4, Pallas kernels, to_scatter(): pl.pallas_call(kernel, in_specs=[VMEM] * len(pieces) + [source.in_spec] +...  30.4 us
    ppermute x12, starting transfers between devices, ring(): return lax.ppermute(value, 'col', self.ring_pairs)  23.9 us
    ppermute x16, starting transfers between devices, exchange(): return lax.ppermute(value, ('row', 'col'), pairs)  18.6 us
    ppermute x12, waiting for transfers between devices, ring(): return lax.ppermute(value, 'col', self.ring_pairs)  7.1 us
    pallas_call x1, Pallas kernels, stage(): pl.pallas_call(kernel, in_specs=[ANY] * (1 + len(after)), out_specs=[VMEM...  6.38 us
  transfers between devices with their start and end apart: 40, of which 13 were waited for; matrix products, arithmetic and copies ran while one was open for 4% of the time, Pallas kernels for 50%

commit v1 on v0

--- a/solution.py
+++ b/solution.py
@@ -387,9 +387,14 @@
 
         @pl.when(pl.program_id(0) == 0)
         def _():
-            ones = jnp.ones((16, tokens), bf16)
-            total = sum(jnp.dot(ones, ref[...], preferred_element_type=f32) for ref in right_refs)
-            refs[-2][...] = total[:8]
+            if part == 0:
+                ones = jnp.ones((16, tokens), bf16)
+                total = sum(
+                    jnp.dot(ones, ref[...], preferred_element_type=f32) for ref in right_refs
+                )
+                refs[-2][...] = total[:8]
+            else:
+                refs[-2][...] = jnp.zeros_like(refs[-2])
             token_ref[...] = jnp.zeros_like(token_ref)
 
         total = sum(

time: 202 us -> 201 us (level)
  transfers between devices with their start and end apart: 40 -> 40, of which waited for: 13 -> 13; matrix products, arithmetic and copies ran while one was open for 4% -> 4% of each run, Pallas kernels for 50% -> 49%
where the time goes in v1:
time: 201 us
  Pallas kernels  98.8 us (49%)
  waiting for transfers between devices  45.7 us (23%)
  starting transfers between devices  43.6 us (22%)
  other arithmetic  7.52 us (4%)
  local copies, waits for them, and re-layouts  4.21 us (2%)
    ppermute x16, waiting for transfers between devices, exchange(): return lax.ppermute(value, ('row', 'col'), pairs)  38 us
    pallas_call x4, Pallas kernels, to_send(): pl.pallas_call(kernel, in_specs=[VMEM] * len(units) + [source.in_spec] +...  31.7 us
    pallas_call x4, Pallas kernels, to_scatter(): pl.pallas_call(kernel, in_specs=[VMEM] * len(pieces) + [source.in_spec] +...  30.4 us
    pallas_call x4, Pallas kernels, weight_grad(): pl.pallas_call(kernel, grid=(steps,), in_specs=[pl.BlockSpec((tokens, wid...  30.3 us
    ppermute x12, starting transfers between devices, ring(): return lax.ppermute(value, 'col', self.ring_pairs)  23.9 us
    ppermute x16, starting transfers between devices, exchange(): return lax.ppermute(value, ('row', 'col'), pairs)  18.6 us
    ppermute x12, waiting for transfers between devices, ring(): return lax.ppermute(value, 'col', self.ring_pairs)  7.62 us
    pallas_call x1, Pallas kernels, stage(): pl.pallas_call(kernel, in_specs=[ANY] * (1 + len(after)), out_specs=[VMEM...  6.38 us
  transfers between devices with their start and end apart: 40, of which 13 were waited for; matrix products, arithmetic and copies ran while one was open for 4% of the time, Pallas kernels for 49%

profile of v1, /device:TPU:0, one launch (start us, length us, event | category | flops | bytes accessed | tf_op | source)
XLA Modules:
  0.0 200.8 jit_solution(16006263461595262890)
XLA Ops:
  0.7 4.1 %collective-permute-start.1 = (bf16[64,3072]{1,0:T(8,128)(2,1)}, bf16[64,3072]{1,0:T(8,128)(2,1)S(1)}, u32[]{:S(2)}, u32[]{:S(2)}) collective-permute-start(bf16[64,3072]{1,0:T(8,128)(2,1)} %refs_0_.2), channel_id=1, source_target_pairs={{0,4},{1,5},{4,6},{5,7},{6,2},{7,3},{2,0},{3,1},{8,12},{9,13},{12,... | collective-permute-start | bytes 1179656 | tf_op jit(solution)/shard_map/ppermute | solution.py:40
  4.7 6.4 %stage_weight.1 = (bf16[3072,3072]{1,0:T(8,128)(2,1)S(1)}, f32[8,128]{1,0:T(8,128)S(1)}) custom-call(bf16[3072,3072]{1,0:T(8,128)(2,1)} %refs_3_.3), custom_call_target="tpu_custom_call" | custom-call | bytes 18874368 | tf_op jit(solution)/shard_map/stage_weight/pallas_call | solution.py:202
  13.9 3.3 %collective-permute-start.5 = (bf16[64,3072]{1,0:T(8,128)(2,1)S(1)}, bf16[64,3072]{1,0:T(8,128)(2,1)S(1)}, u32[]{:S(2)}, u32[]{:S(2)}) collective-permute-start(bf16[64,3072]{1,0:T(8,128)(2,1)S(1)} %copy-done.9), channel_id=1, source_target_pairs={{0,4},{1,5},{4,6},{5,7},{6,2},{7,3},{2,0},{3,1},{8,12},{9,13},{12,... | collective-permute-start | bytes 1179656 | tf_op jit(solution)/shard_map/ppermute | solution.py:40
  17.2 6.1 %product_to_send.4 = (bf16[256,3072]{1,0:T(8,128)(2,1)}, f32[128,3072]{1,0:T(8,128)S(1)}, bf16[128,3072]{1,0:T(8,128)(2,1)S(1)}, f32[8,128]{1,0:T(8,128)S(1)}) custom-call(bf16[64,3072]{1,0:T(8,128)(2,1)S(1)} %copy-done.8, bf16[64,3072]{1,0:T(8,128)(2,1)S(1)} %collective-permute-done.refs_1_, bf16[64,3072]{1,0:T(8,128)(2,1)S(1)} %collective-permute-done.1.refs_2_, ...), custom_call_target="tpu_custom_call" | custom-call | flops 4831838208 | bytes 8388608 | tf_op jit(solution)/shard_map/product_to_send/pallas_call | solution.py:293
  23.3 2.4 %collective-permute-done.5.refs_2_ = bf16[64,3072]{1,0:T(8,128)(2,1)S(1)} collective-permute-done((bf16[64,3072]{1,0:T(8,128)(2,1)S(1)}, bf16[64,3072]{1,0:T(8,128)(2,1)S(1)}, u32[]{:S(2)}, u32[]{:S(2)}) %collective-permute-start.5) | collective-permute-done | bytes 393248 | tf_op jit(solution)/shard_map/ppermute | solution.py:40
  27.3 3.4 %collective-permute-start.8 = (bf16[64,3072]{1,0:T(8,128)(2,1)S(1)}, bf16[64,3072]{1,0:T(8,128)(2,1)S(1)}, u32[]{:S(2)}, u32[]{:S(2)}) collective-permute-start(bf16[64,3072]{1,0:T(8,128)(2,1)S(1)} %collective-permute-done.1.refs_2_), channel_id=1, source_target_pairs={{0,4},{1,5},{4,6},{5,7},{6,2},{7,3},{2,0},{3,1},{8,12},{9,13},{12,... | collective-permute-start | bytes 1179656 | tf_op jit(solution)/shard_map/ppermute | solution.py:40
  30.6 8.6 %product_to_send.5 = (bf16[256,3072]{1,0:T(8,128)(2,1)}, f32[128,3072]{1,0:T(8,128)S(1)}, bf16[128,3072]{1,0:T(8,128)(2,1)S(1)}, f32[8,128]{1,0:T(8,128)S(1)}) custom-call(bf16[64,3072]{1,0:T(8,128)(2,1)S(1)} %copy-done.9, bf16[64,3072]{1,0:T(8,128)(2,1)S(1)} %collective-permute-done.4.refs_1_, bf16[64,3072]{1,0:T(8,128)(2,1)S(1)} %collective-permute-done.5.refs_2_, ...), custom_call_target="tpu_custom_call" | custom-call | flops 4831838208 | bytes 8388608 | tf_op jit(solution)/shard_map/product_to_send/pallas_call | solution.py:293
  41.6 2.8 %collective-permute-start.11 = (bf16[64,3072]{1,0:T(8,128)(2,1)S(1)}, bf16[64,3072]{1,0:T(8,128)(2,1)S(1)}, u32[]{:S(2)}, u32[]{:S(2)}) collective-permute-start(bf16[64,3072]{1,0:T(8,128)(2,1)S(1)} %collective-permute-done.5.refs_2_), channel_id=1, source_target_pairs={{0,4},{1,5},{4,6},{5,7},{6,2},{7,3},{2,0},{3,1},{8,12},{9,13},{12,... | collective-permute-start | bytes 1179656 | tf_op jit(solution)/shard_map/ppermute | solution.py:40
  44.5 6.8 %collective-permute-done.7 = bf16[64,3072]{1,0:T(8,128)(2,1)S(1)} collective-permute-done((bf16[64,3072]{1,0:T(8,128)(2,1)S(1)}, bf16[64,3072]{1,0:T(8,128)(2,1)S(1)}, u32[]{:S(2)}, u32[]{:S(2)}) %collective-permute-start.7) | collective-permute-done | bytes 393248 | tf_op jit(solution)/shard_map/ppermute | solution.py:51
  53.4 4.3 %collective-permute-done.10 = bf16[128,3072]{1,0:T(8,128)(2,1)S(1)} collective-permute-done((bf16[128,3072]{1,0:T(8,128)(2,1)S(1)}, bf16[128,3072]{1,0:T(8,128)(2,1)S(1)}, u32[]{:S(2)}, u32[]{:S(2)}) %collective-permute-start.10) | collective-permute-done | bytes 786464 | tf_op jit(solution)/shard_map/ppermute | solution.py:51
  60.9 3.0 %collective-permute-start.14 = (bf16[64,3072]{1,0:T(8,128)(2,1)S(1)}, bf16[64,3072]{1,0:T(8,128)(2,1)S(1)}, u32[]{:S(2)}, u32[]{:S(2)}) collective-permute-start(bf16[64,3072]{1,0:T(8,128)(2,1)S(1)} %collective-permute-done.11.refs_0_), channel_id=1, source_target_pairs={{0,4},{1,5},{4,6},{5,7},{6,2},{7,3},{2,0},{3,1},{8,12},{9,13},{12,... | collective-permute-start | bytes 1179656 | tf_op jit(solution)/shard_map/ppermute | solution.py:40
  64.4 8.5 %product_to_send.6 = (bf16[256,3072]{1,0:T(8,128)(2,1)}, f32[128,3072]{1,0:T(8,128)S(1)}, bf16[128,3072]{1,0:T(8,128)(2,1)S(1)}, f32[8,128]{1,0:T(8,128)S(1)}) custom-call(bf16[64,3072]{1,0:T(8,128)(2,1)S(1)} %collective-permute-done.8.refs_0_, bf16[64,3072]{1,0:T(8,128)(2,1)S(1)} %collective-permute-done.15.refs_1_, ...), custom_call_target="tpu_custom_call" | custom-call | flops 4831838208 | bytes 8388608 | tf_op jit(solution)/shard_map/product_to_send/pallas_call | solution.py:293
  77.6 6.7 %collective-permute-done.20.refs_1_ = bf16[64,3072]{1,0:T(8,128)(2,1)S(1)} collective-permute-done((bf16[64,3072]{1,0:T(8,128)(2,1)S(1)}, bf16[64,3072]{1,0:T(8,128)(2,1)S(1)}, u32[]{:S(2)}, u32[]{:S(2)}) %collective-permute-start.20) | collective-permute-done | bytes 393248 | tf_op jit(solution)/shard_map/ppermute | solution.py:51
  86.2 8.6 %product_to_send.7 = (bf16[256,3072]{1,0:T(8,128)(2,1)}, f32[128,3072]{1,0:T(8,128)S(1)}, bf16[128,3072]{1,0:T(8,128)(2,1)S(1)}, f32[8,128]{1,0:T(8,128)S(1)}, bf16[3072,3072]{1,0:T(8,128)(2,1)S(1)}) custom-call(bf16[64,3072]{1,0:T(8,128)(2,1)S(1)} %collective-permute-done.11.refs_0_, bf16[64,3072]{1,0:T(8,128)(2,1)S(1)} %collective-permute-done.13.refs_1_, ...), custom_call_target="tpu_custom_call" | custom-call | flops 4831838208 | bytes 8388608 | tf_op jit(solution)/shard_map/product_to_send/pallas_call | solution.py:293
  98.6 6.3 %product_to_scatter.4 = (bf16[256,3072]{1,0:T(8,128)(2,1)}, f32[128,3072]{1,0:T(8,128)S(1)}, bf16[128,3072]{1,0:T(8,128)(2,1)S(1)}, f32[8,128]{1,0:T(8,128)S(1)}) custom-call(bf16[64,3072]{1,0:T(8,128)(2,1)S(1)} %multiply_convert_fusion.1.refs_0_, bf16[64,3072]{1,0:T(8,128)(2,1)S(1)} %collective-permute-done.9.refs_1_, ...), custom_call_target="tpu_custom_call" | custom-call | flops 4831838208 | bytes 8388608 | tf_op jit(solution)/shard_map/product_to_scatter/pallas_call | solution.py:353
  105.0 4.6 %collective-permute-done.22 = bf16[64,3072]{1,0:T(8,128)(2,1)S(1)} collective-permute-done((bf16[64,3072]{1,0:T(8,128)(2,1)S(1)}, bf16[64,3072]{1,0:T(8,128)(2,1)S(1)}, u32[]{:S(2)}, u32[]{:S(2)}) %collective-permute-start.22) | collective-permute-done | bytes 393248 | tf_op jit(solution)/shard_map/ppermute | solution.py:51
  111.1 8.9 %product_to_scatter.5 = (bf16[256,3072]{1,0:T(8,128)(2,1)}, f32[128,3072]{1,0:T(8,128)S(1)}, bf16[128,3072]{1,0:T(8,128)(2,1)S(1)}, f32[8,128]{1,0:T(8,128)S(1)}) custom-call(bf16[64,3072]{1,0:T(8,128)(2,1)S(1)} %fusion.6.refs_0_, bf16[64,3072]{1,0:T(8,128)(2,1)S(1)} %collective-permute-done.20.refs_1_, ...), custom_call_target="tpu_custom_call" | custom-call | flops 4831838208 | bytes 8388608 | tf_op jit(solution)/shard_map/product_to_scatter/pallas_call | solution.py:353
  127.9 8.0 %collective-permute-done.29 = bf16[64,3072]{1,0:T(8,128)(2,1)S(1)} collective-permute-done((bf16[64,3072]{1,0:T(8,128)(2,1)S(1)}, bf16[64,3072]{1,0:T(8,128)(2,1)S(1)}, u32[]{:S(2)}, u32[]{:S(2)}) %collective-permute-start.29) | collective-permute-done | bytes 393248 | tf_op jit(solution)/shard_map/ppermute | solution.py:51
  138.7 6.3 %product_to_scatter.6 = (bf16[256,3072]{1,0:T(8,128)(2,1)}, f32[128,3072]{1,0:T(8,128)S(1)}, bf16[128,3072]{1,0:T(8,128)(2,1)S(1)}, f32[8,128]{1,0:T(8,128)S(1)}) custom-call(bf16[64,3072]{1,0:T(8,128)(2,1)S(1)} %multiply_convert_fusion.refs_0_, bf16[64,3072]{1,0:T(8,128)(2,1)S(1)} %collective-permute-done.25.refs_1_, ...), custom_call_target="tpu_custom_call" | custom-call | flops 4831838208 | bytes 8388608 | tf_op jit(solution)/shard_map/product_to_scatter/pallas_call | solution.py:353
  149.3 7.8 %weight_grad.4 = (bf16[3072,3072]{1,0:T(8,128)(2,1)}, f32[8,3072]{1,0:T(8,128)S(1)}, f32[8,128]{1,0:T(8,128)S(1)}) custom-call(bf16[256,3072]{1,0:T(8,128)(2,1)S(1)} %copy-done.5, bf16[256,3072]{1,0:T(8,128)(2,1)S(1)} %copy-done.6, bf16[256,3072]{1,0:T(8,128)(2,1)S(1)} %copy-done.1, bf16[256,3072]{1,0:T(8,128)(2,1)S(1)} %copy-done.3, ...), custom_call_target="tpu_custom_call" | custom-call | flops 4831838208 | bytes 9437184 | tf_op jit(solution)/shard_map/weight_grad/pallas_call | solution.py:409
  158.9 8.9 %product_to_scatter.7 = (bf16[256,3072]{1,0:T(8,128)(2,1)}, f32[128,3072]{1,0:T(8,128)S(1)}, bf16[128,3072]{1,0:T(8,128)(2,1)S(1)}, f32[8,128]{1,0:T(8,128)S(1)}) custom-call(bf16[64,3072]{1,0:T(8,128)(2,1)S(1)} %fusion.13.refs_0_, bf16[64,3072]{1,0:T(8,128)(2,1)S(1)} %collective-permute-done.30.refs_1_, ...), custom_call_target="tpu_custom_call" | custom-call | flops 4831838208 | bytes 8388608 | tf_op jit(solution)/shard_map/product_to_scatter/pallas_call | solution.py:353
  171.3 7.3 %weight_grad.5 = (bf16[3072,3072]{1,0:T(8,128)(2,1)}, f32[8,3072]{1,0:T(8,128)}, f32[8,128]{1,0:T(8,128)S(1)}) custom-call(bf16[256,3072]{1,0:T(8,128)(2,1)S(1)} %copy-done.5, bf16[256,3072]{1,0:T(8,128)(2,1)S(1)} %copy-done.6, bf16[256,3072]{1,0:T(8,128)(2,1)S(1)} %copy-done.1, bf16[256,3072]{1,0:T(8,128)(2,1)S(1)} %copy-done.3, ...), custom_call_target="tpu_custom_call", output_to_operand_aliasing={{0}: (5, {})} | custom-call | flops 4831838208 | bytes 9437184 | tf_op jit(solution)/shard_map/weight_grad/pallas_call | solution.py:409
  181.1 7.8 %weight_grad.6 = (bf16[3072,3072]{1,0:T(8,128)(2,1)}, f32[8,3072]{1,0:T(8,128)S(1)}, f32[8,128]{1,0:T(8,128)S(1)}) custom-call(bf16[256,3072]{1,0:T(8,128)(2,1)S(1)} %copy-done, bf16[256,3072]{1,0:T(8,128)(2,1)S(1)} %copy-done.2, bf16[256,3072]{1,0:T(8,128)(2,1)S(1)} %copy-done.4, bf16[256,3072]{1,0:T(8,128)(2,1)S(1)} %copy-done.7, ...), custom_call_target="tpu_custom_call" | custom-call | flops 4831838208 | bytes 9437184 | tf_op jit(solution)/shard_map/weight_grad/pallas_call | solution.py:409
  192.7 7.3 %weight_grad.7 = (bf16[3072,3072]{1,0:T(8,128)(2,1)}, f32[8,3072]{1,0:T(8,128)}, f32[8,128]{1,0:T(8,128)}) custom-call(bf16[256,3072]{1,0:T(8,128)(2,1)S(1)} %copy-done, bf16[256,3072]{1,0:T(8,128)(2,1)S(1)} %copy-done.2, bf16[256,3072]{1,0:T(8,128)(2,1)S(1)} %copy-done.4, bf16[256,3072]{1,0:T(8,128)(2,1)S(1)} %copy-done.7, ...), custom_call_target="tpu_custom_call", output_to_operand_aliasing={{0}: (5, {})} | custom-call | flops 4831838208 | bytes 9437184 | tf_op jit(solution)/shard_map/weight_grad/pallas_call | solution.py:409
  (125 shorter events, 51.6 us)
Async XLA Ops:
  0.7 12.8 %collective-permute-start.1 = (bf16[64,3072]{1,0:T(8,128)(2,1)}, bf16[64,3072]{1,0:T(8,128)(2,1)S(1)}, u32[]{:S(2)}, u32[]{:S(2)}) collective-permute-start(bf16[64,3072]{1,0:T(8,128)(2,1)} %refs_0_.2), channel_id=1, source_target_pairs={{0,4},{1,5},{4,6},{5,7},{6,2},{7,3},{2,0},{3,1},{8,12},{9,13},{12,... | collective-permute-start | bytes 1179656 | tf_op jit(solution)/shard_map/ppermute | solution.py:40
  4.7 12.5 %collective-permute-start = (bf16[64,3072]{1,0:T(8,128)(2,1)}, bf16[64,3072]{1,0:T(8,128)(2,1)S(1)}, u32[]{:S(2)}, u32[]{:S(2)}) collective-permute-start(bf16[64,3072]{1,0:T(8,128)(2,1)} %refs_0_.2), channel_id=1, source_target_pairs={{0,1},{1,0},{2,3},{3,2},{4,5},{5,4},{6,7},{7,6},{8,9},{9,8},{10,11... | collective-permute-start | bytes 1179656 | tf_op jit(solution)/shard_map/ppermute | solution.py:43
  13.4 17.2 %collective-permute-start.4 = (bf16[64,3072]{1,0:T(8,128)(2,1)S(1)}, bf16[64,3072]{1,0:T(8,128)(2,1)S(1)}, u32[]{:S(2)}, u32[]{:S(2)}) collective-permute-start(bf16[64,3072]{1,0:T(8,128)(2,1)S(1)} %copy-done.9), channel_id=1, source_target_pairs={{0,1},{1,0},{2,3},{3,2},{4,5},{5,4},{6,7},{7,6},{8,9},{9,8},{10,11... | collective-permute-start | bytes 1179656 | tf_op jit(solution)/shard_map/ppermute | solution.py:43
  25.8 13.5 %collective-permute-start.3 = (bf16[128,3072]{1,0:T(8,128)(2,1)S(1)}, bf16[128,3072]{1,0:T(8,128)(2,1)S(1)}, u32[]{:S(2)}, u32[]{:S(2)}) collective-permute-start(bf16[128,3072]{1,0:T(8,128)(2,1)S(1)} %get-tuple-element.121), channel_id=1, source_target_pairs={{0,8},{1,17},{2,10},{3,19},{4,12},{5,21},{6,14},{7,23},{8,0},{9,25... | collective-permute-start | bytes 2359304 | tf_op jit(solution)/shard_map/ppermute | solution.py:51
  27.3 17.2 %collective-permute-start.8 = (bf16[64,3072]{1,0:T(8,128)(2,1)S(1)}, bf16[64,3072]{1,0:T(8,128)(2,1)S(1)}, u32[]{:S(2)}, u32[]{:S(2)}) collective-permute-start(bf16[64,3072]{1,0:T(8,128)(2,1)S(1)} %collective-permute-done.1.refs_2_), channel_id=1, source_target_pairs={{0,4},{1,5},{4,6},{5,7},{6,2},{7,3},{2,0},{3,1},{8,12},{9,13},{12,... | collective-permute-start | bytes 1179656 | tf_op jit(solution)/shard_map/ppermute | solution.py:40
  41.1 16.6 %collective-permute-start.10 = (bf16[128,3072]{1,0:T(8,128)(2,1)S(1)}, bf16[128,3072]{1,0:T(8,128)(2,1)S(1)}, u32[]{:S(2)}, u32[]{:S(2)}) collective-permute-start(bf16[128,3072]{1,0:T(8,128)(2,1)S(1)} %get-tuple-element.133), channel_id=1, source_target_pairs={{0,8},{1,17},{2,10},{3,19},{4,12},{5,21},{6,14},{7,23},{8,0},{9,25... | collective-permute-start | bytes 2359304 | tf_op jit(solution)/shard_map/ppermute | solution.py:51
  41.6 16.3 %collective-permute-start.11 = (bf16[64,3072]{1,0:T(8,128)(2,1)S(1)}, bf16[64,3072]{1,0:T(8,128)(2,1)S(1)}, u32[]{:S(2)}, u32[]{:S(2)}) collective-permute-start(bf16[64,3072]{1,0:T(8,128)(2,1)S(1)} %collective-permute-done.5.refs_2_), channel_id=1, source_target_pairs={{0,4},{1,5},{4,6},{5,7},{6,2},{7,3},{2,0},{3,1},{8,12},{9,13},{12,... | collective-permute-start | bytes 1179656 | tf_op jit(solution)/shard_map/ppermute | solution.py:40
  44.4 19.9 %collective-permute-start.15 = (bf16[64,3072]{1,0:T(8,128)(2,1)S(1)}, bf16[64,3072]{1,0:T(8,128)(2,1)S(1)}, u32[]{:S(2)}, u32[]{:S(2)}) collective-permute-start(bf16[64,3072]{1,0:T(8,128)(2,1)S(1)} %collective-permute-done.8.refs_0_), channel_id=1, source_target_pairs={{0,1},{1,0},{2,3},{3,2},{4,5},{5,4},{6,7},{7,6},{8,9},{9,8},{10,11... | collective-permute-start | bytes 1179656 | tf_op jit(solution)/shard_map/ppermute | solution.py:43
  44.4 16.5 %collective-permute-start.16 = (bf16[64,3072]{1,0:T(8,128)(2,1)S(1)}, bf16[64,3072]{1,0:T(8,128)(2,1)S(1)}, u32[]{:S(2)}, u32[]{:S(2)}) collective-permute-start(bf16[64,3072]{1,0:T(8,128)(2,1)S(1)} %collective-permute-done.8.refs_0_), channel_id=1, source_target_pairs={{0,4},{1,5},{4,6},{5,7},{6,2},{7,3},{2,0},{3,1},{8,12},{9,13},{12,... | collective-permute-start | bytes 1179656 | tf_op jit(solution)/shard_map/ppermute | solution.py:40
  60.9 14.2 %collective-permute-start.14 = (bf16[64,3072]{1,0:T(8,128)(2,1)S(1)}, bf16[64,3072]{1,0:T(8,128)(2,1)S(1)}, u32[]{:S(2)}, u32[]{:S(2)}) collective-permute-start(bf16[64,3072]{1,0:T(8,128)(2,1)S(1)} %collective-permute-done.11.refs_0_), channel_id=1, source_target_pairs={{0,4},{1,5},{4,6},{5,7},{6,2},{7,3},{2,0},{3,1},{8,12},{9,13},{12,... | collective-permute-start | bytes 1179656 | tf_op jit(solution)/shard_map/ppermute | solution.py:40
  75.6 23.0 %collective-permute-start.12 = (bf16[128,3072]{1,0:T(8,128)(2,1)}, bf16[128,3072]{1,0:T(8,128)(2,1)S(1)}, u32[]{:S(2)}, u32[]{:S(2)}) collective-permute-start(bf16[128,3072]{1,0:T(8,128)(2,1)} %pad_maximum_fusion), channel_id=1, source_target_pairs={{0,8},{1,17},{2,10},{3,19},{4,12},{5,21},{6,14},{7,23},{8,0},{9,25... | collective-permute-start | bytes 2359304 | tf_op jit(solution)/shard_map/ppermute | solution.py:51
  76.1 21.1 %collective-permute-start.21 = (bf16[128,3072]{1,0:T(8,128)(2,1)S(1)}, bf16[128,3072]{1,0:T(8,128)(2,1)S(1)}, u32[]{:S(2)}, u32[]{:S(2)}) collective-permute-start(bf16[128,3072]{1,0:T(8,128)(2,1)S(1)} %get-tuple-element.151), channel_id=1, source_target_pairs={{0,8},{1,17},{2,10},{3,19},{4,12},{5,21},{6,14},{7,23},{8,0},{9,25... | collective-permute-start | bytes 2359304 | tf_op jit(solution)/shard_map/ppermute | solution.py:51
  84.4 26.7 %collective-permute-start.24 = (bf16[128,3072]{1,0:T(8,128)(2,1)S(1)}, bf16[128,3072]{1,0:T(8,128)(2,1)S(1)}, u32[]{:S(2)}, u32[]{:S(2)}) collective-permute-start(bf16[128,3072]{1,0:T(8,128)(2,1)S(1)} %pad_maximum_fusion.1), channel_id=1, source_target_pairs={{0,8},{1,17},{2,10},{3,19},{4,12},{5,21},{6,14},{7,23},{8,0},{9,25... | collective-permute-start | bytes 2359304 | tf_op jit(solution)/shard_map/ppermute | solution.py:51
  94.8 28.8 %collective-permute-start.26 = (bf16[128,3072]{1,0:T(8,128)(2,1)S(1)}, bf16[128,3072]{1,0:T(8,128)(2,1)S(1)}, u32[]{:S(2)}, u32[]{:S(2)}) collective-permute-start(bf16[128,3072]{1,0:T(8,128)(2,1)S(1)} %get-tuple-element.168), channel_id=1, source_target_pairs={{0,8},{1,17},{2,10},{3,19},{4,12},{5,21},{6,14},{7,23},{8,0},{9,25... | collective-permute-start | bytes 2359304 | tf_op jit(solution)/shard_map/ppermute | solution.py:51
  97.4 12.1 %collective-permute-start.22 = (bf16[64,3072]{1,0:T(8,128)(2,1)S(1)}, bf16[64,3072]{1,0:T(8,128)(2,1)S(1)}, u32[]{:S(2)}, u32[]{:S(2)}) collective-permute-start(bf16[64,3072]{1,0:T(8,128)(2,1)S(1)} %slice.143), channel_id=1, source_target_pairs={{0,16},{1,9},{2,18},{3,11},{4,20},{5,13},{6,22},{7,15},{8,24},{9,1... | collective-permute-start | bytes 1179656 | tf_op jit(solution)/shard_map/ppermute | solution.py:51
  109.9 12.1 %collective-permute-start.25 = (bf16[64,3072]{1,0:T(8,128)(2,1)S(1)}, bf16[64,3072]{1,0:T(8,128)(2,1)S(1)}, u32[]{:S(2)}, u32[]{:S(2)}) collective-permute-start(bf16[64,3072]{1,0:T(8,128)(2,1)S(1)} %multiply_convert_fusion.refs_0_), channel_id=1, source_target_pairs={{0,16},{1,9},{2,18},{3,11},{4,20},{5,13},{6,22},{7,15},{8,24},{9,1... | collective-permute-start | bytes 1179656 | tf_op jit(solution)/shard_map/ppermute | solution.py:51
  111.1 13.3 %collective-permute-start.23 = (bf16[128,3072]{1,0:T(8,128)(2,1)S(1)}, bf16[128,3072]{1,0:T(8,128)(2,1)S(1)}, u32[]{:S(2)}, u32[]{:S(2)}) collective-permute-start(bf16[128,3072]{1,0:T(8,128)(2,1)S(1)} %get-tuple-element.161), channel_id=1, source_target_pairs={{0,1},{1,0},{2,3},{3,2},{4,5},{5,4},{6,7},{7,6},{8,9},{9,8},{10,11... | collective-permute-start | bytes 2359304 | tf_op jit(solution)/shard_map/ppermute | solution.py:43
  122.1 16.6 %collective-permute-start.28 = (bf16[128,3072]{1,0:T(8,128)(2,1)S(1)}, bf16[128,3072]{1,0:T(8,128)(2,1)S(1)}, u32[]{:S(2)}, u32[]{:S(2)}) collective-permute-start(bf16[128,3072]{1,0:T(8,128)(2,1)S(1)} %pad_maximum_fusion.2), channel_id=1, source_target_pairs={{0,8},{1,17},{2,10},{3,19},{4,12},{5,21},{6,14},{7,23},{8,0},{9,25... | collective-permute-start | bytes 2359304 | tf_op jit(solution)/shard_map/ppermute | solution.py:51
  123.8 12.1 %collective-permute-start.29 = (bf16[64,3072]{1,0:T(8,128)(2,1)S(1)}, bf16[64,3072]{1,0:T(8,128)(2,1)S(1)}, u32[]{:S(2)}, u32[]{:S(2)}) collective-permute-start(bf16[64,3072]{1,0:T(8,128)(2,1)S(1)} %slice.142), channel_id=1, source_target_pairs={{0,16},{1,9},{2,18},{3,11},{4,20},{5,13},{6,22},{7,15},{8,24},{9,1... | collective-permute-start | bytes 1179656 | tf_op jit(solution)/shard_map/ppermute | solution.py:51
  126.7 20.3 %collective-permute-start.27 = (bf16[64,3072]{1,0:T(8,128)(2,1)S(1)}, bf16[64,3072]{1,0:T(8,128)(2,1)S(1)}, u32[]{:S(2)}, u32[]{:S(2)}) collective-permute-start(bf16[64,3072]{1,0:T(8,128)(2,1)S(1)} %slice.141), channel_id=1, source_target_pairs={{0,4},{1,5},{4,6},{5,7},{6,2},{7,3},{2,0},{3,1},{8,12},{9,13},{12,... | collective-permute-start | bytes 1179656 | tf_op jit(solution)/shard_map/ppermute | solution.py:40
  127.9 19.0 %collective-permute-start.32 = (bf16[128,3072]{1,0:T(8,128)(2,1)S(1)}, bf16[128,3072]{1,0:T(8,128)(2,1)S(1)}, u32[]{:S(2)}, u32[]{:S(2)}) collective-permute-start(bf16[128,3072]{1,0:T(8,128)(2,1)S(1)} %get-tuple-element.190), channel_id=1, source_target_pairs={{0,1},{1,0},{2,3},{3,2},{4,5},{5,4},{6,7},{7,6},{8,9},{9,8},{10,11... | collective-permute-start | bytes 2359304 | tf_op jit(solution)/shard_map/ppermute | solution.py:43
  145.1 12.1 %collective-permute-start.33 = (bf16[128,3072]{1,0:T(8,128)(2,1)S(1)}, bf16[128,3072]{1,0:T(8,128)(2,1)S(1)}, u32[]{:S(2)}, u32[]{:S(2)}) collective-permute-start(bf16[128,3072]{1,0:T(8,128)(2,1)S(1)} %pad_maximum_fusion.3), channel_id=1, source_target_pairs={{0,8},{1,17},{2,10},{3,19},{4,12},{5,21},{6,14},{7,23},{8,0},{9,25... | collective-permute-start | bytes 2359304 | tf_op jit(solution)/shard_map/ppermute | solution.py:51
  147.2 20.6 %collective-permute-start.35 = (bf16[64,3072]{1,0:T(8,128)(2,1)S(1)}, bf16[64,3072]{1,0:T(8,128)(2,1)S(1)}, u32[]{:S(2)}, u32[]{:S(2)}) collective-permute-start(bf16[64,3072]{1,0:T(8,128)(2,1)S(1)} %slice.140), channel_id=1, source_target_pairs={{0,4},{1,5},{4,6},{5,7},{6,2},{7,3},{2,0},{3,1},{8,12},{9,13},{12,... | collective-permute-start | bytes 1179656 | tf_op jit(solution)/shard_map/ppermute | solution.py:40
  170.5 19.9 %collective-permute-start.38 = (bf16[64,3072]{1,0:T(8,128)(2,1)S(1)}, bf16[64,3072]{1,0:T(8,128)(2,1)S(1)}, u32[]{:S(2)}, u32[]{:S(2)}) collective-permute-start(bf16[64,3072]{1,0:T(8,128)(2,1)S(1)} %fusion.18), channel_id=1, source_target_pairs={{0,4},{1,5},{4,6},{5,7},{6,2},{7,3},{2,0},{3,1},{8,12},{9,13},{12,... | collective-permute-start | bytes 1179656 | tf_op jit(solution)/shard_map/ppermute | solution.py:40
  (29 other events, 238.3 us)
